TPU v7x, 512 devices: a whole 4x4x16 slice. The times are simulated.
512 devices in a mesh: lat: 128 (over x, z, core), lev: 4 (over y).
Axes of the slice: x: 4, y: 4, z: 16, core: 2. Of those that a mesh axis runs over, the one named last changes fastest.
Arguments:
- spec_in: bfloat16 [128, 192, 1280], P('lat', 'lev'), may hold values from -6 to 6
- legendre: bfloat16 [128, 512, 1280], P('lat'), may hold values from -0.15625 to 0.15625
- wavenum: int32 [128], replicated, may hold values from 0 to 1279, as said below
- counts: int32 [512], P('lat'), may hold values from 3856 to 5136, as said below
- quad_weights: float32 [512], P('lat'), may hold values from 1 to 4
- vert_in: float32 [32, 32], P(None, 'lev'), may hold values from -1 to 1
- vert_out: float32 [32, 32], P('lev'), may hold values from -1 to 1
- mode_rates: float32 [32], replicated, may hold values from 0.1 to 10
Outputs:
- spec_out: bfloat16 [128, 192, 1280], P('lat', 'lev')
Inputs may be any that keep to these rules, and one draw needn't show every extreme that they name: `wavenum`: 128 distinct wavenumbers below 1280; 0 and 1279 are among them. `counts`: each count is 20 + 4 k for a whole k; the first latitude has 5136 points.
All inputs are finite; a program needn't handle non-finite values.
Results may differ from a plain program's by a relative error of at most 0.0054.
Values may be sent and summed in bfloat16 or wider, within the bound.
A program may use at most 64 MiB of HBM per device.

v0:
```python
import math

import jax
import jax.numpy as jnp
from jax import lax
from jax.sharding import PartitionSpec as P

PTS = 5136
FIELDS = 3


full_turn = 2.0 * math.pi


def trig_rows(wavenum, point_count):
    points = jnp.arange(PTS, dtype=jnp.int32)
    phases = wavenum[:, None] * points[None, :] % point_count
    angles = phases.astype(jnp.float32) * (full_turn / point_count.astype(jnp.float32))
    inside = points[None, :] < point_count
    cosine = jnp.where(inside, jnp.cos(angles), 0.0)
    sine_rows = jnp.where(inside, jnp.sin(angles), 0.0)
    return jnp.concatenate([cosine, sine_rows], 0).astype(jnp.bfloat16)


def grid_step(coeffs, wavenum, point_count, weight):
    wave_count = coeffs.shape[0]
    row_count = coeffs.shape[1] // 2
    trig_table = trig_rows(wavenum, point_count)
    paired = coeffs.reshape(wave_count, row_count, 2)
    stacked = jnp.concatenate([paired[:, :, 0], paired[:, :, 1]], 0)
    fields = lax.dot_general(
        stacked, trig_table, (((0,), (0,)), ((), ())), preferred_element_type=jnp.float32
    )
    fields = fields * (1.0 / math.sqrt(2 * wave_count))
    levels = fields.reshape(row_count // FIELDS, FIELDS, PTS)
    diverg_grid = levels[:, 0]
    wind_grid = levels[:, 1]
    temp_grid = levels[:, 2]
    tendency = jnp.stack(
        [
            diverg_grid - wind_grid * temp_grid,
            wind_grid + diverg_grid * temp_grid,
            temp_grid - diverg_grid * wind_grid,
        ],
        1,
    )
    tendency = tendency.reshape(row_count, PTS).astype(jnp.bfloat16)
    spectra = lax.dot_general(
        tendency, trig_table, (((1,), (1,)), ((), ())), preferred_element_type=jnp.float32
    )
    factor = weight / jnp.sqrt(point_count.astype(jnp.float32))
    cosine = spectra[:, :wave_count] * factor
    sine_part = -spectra[:, wave_count:] * factor
    return (
        jnp.stack([cosine.T, sine_part.T], 2)
        .reshape(wave_count, 2 * row_count)
        .astype(jnp.bfloat16)
    )


def body(spec_in, legendre, wavenum, counts, quad_weights, vert_in, vert_out, mode_rates):
    slot_count = spec_in.shape[0]
    trunc_width = spec_in.shape[2]
    level_count = vert_out.shape[0]
    levels_all = vert_out.shape[1]
    first_slot = lax.axis_index("lat") * slot_count
    local_orders = lax.dynamic_slice_in_dim(wavenum, first_slot, slot_count, 0)
    columns = jnp.arange(trunc_width, dtype=jnp.int32)
    masked = jnp.where(
        columns[None, None, :] >= local_orders[:, None, None], legendre, jnp.zeros_like(legendre)
    )
    fourier = lax.dot_general(
        spec_in, masked, (((2,), (2,)), ((0,), (0,))), preferred_element_type=jnp.float32
    ).astype(jnp.bfloat16)
    latitudes = lax.all_to_all(fourier, "lat", split_axis=2, concat_axis=0, tiled=True)

    def latitude_one(operands):
        coeffs, point_count, weight = operands
        return grid_step(coeffs, wavenum, point_count, weight)

    returned = lax.map(latitude_one, (latitudes.transpose(2, 0, 1), counts, quad_weights))
    returned = returned.transpose(1, 2, 0)
    gathered_back = lax.all_to_all(returned, "lat", split_axis=0, concat_axis=2, tiled=True)
    spectra = lax.dot_general(
        gathered_back, masked, (((2,), (1,)), ((0,), (0,))), preferred_element_type=jnp.float32
    )
    shaped = spectra.reshape(slot_count, level_count, FIELDS, 2, trunc_width)
    diverg = (
        shaped[:, :, 0].transpose(1, 0, 2, 3).reshape(level_count, slot_count * 2 * trunc_width)
    )
    degree = columns.astype(jnp.float32)
    growth = degree * (degree + 1.0) / float(trunc_width * trunc_width)
    partial_modes = jnp.dot(
        vert_in, diverg, precision=lax.Precision.HIGHEST, preferred_element_type=jnp.float32
    )
    mode_values = lax.psum(partial_modes, "lev")
    divisor = 1.0 + mode_rates[:, None] * growth[None, :]
    damped = mode_values.reshape(levels_all, slot_count * 2, trunc_width) / divisor[:, None, :]
    damped = damped.reshape(levels_all, slot_count * 2 * trunc_width)
    solved = jnp.dot(
        vert_out, damped, precision=lax.Precision.HIGHEST, preferred_element_type=jnp.float32
    )
    solved = solved.reshape(level_count, slot_count, 2, trunc_width).transpose(1, 0, 2, 3)
    result = shaped.at[:, :, 0].set(solved)
    return result.reshape(slot_count, 2 * FIELDS * level_count, trunc_width).astype(jnp.bfloat16)


def solution(mesh):
    return jax.shard_map(
        body,
        mesh=mesh,
        in_specs=(
            P("lat", "lev", None),
            P("lat", None, None),
            P(),
            P("lat"),
            P("lat"),
            P(None, "lev"),
            P("lev", None),
            P(),
        ),
        out_specs=P("lat", "lev", None),
        check_vma=False,
    )
```

profile of v0, /device:TPU:1, one launch (start us, length us, event | category | flops | bytes accessed | tf_op | source)
XLA Modules:
  0.0 329.0 jit_solution(3749446744925732384)
XLA Ops:
  6.5 1.3 dynamic_slice.15
  7.8 0.7 iota_compare_fusion.1
  8.5 1.8 fusion.23
  10.3 0.9 copy.24
  11.2 20.4 %all-to-all-start = ((bf16[1,48,512]{1,0,2:T(2,128)(2,1)}), bf16[1,48,512]{1,0,2:T(2,128)(2,1)S(1)}, u32[]{:S(2)}, u32[]{:S(2)}) async-start(bf16[1,48,512]{1,0,2:T(2,128)(2,1)} %copy.24), calls=%async_computation | async-start | bytes 524288 | tf_op jit(solution)/shard_map/all_to_all | solution.py:75
  31.6 22.5 %all-to-all-done = bf16[1,48,512]{1,0,2:T(2,128)(2,1)S(1)} async-done(((bf16[1,48,512]{1,0,2:T(2,128)(2,1)}), bf16[1,48,512]{1,0,2:T(2,128)(2,1)S(1)}, u32[]{:S(2)}, u32[]{:S(2)}) %all-to-all-start) | async-done | bytes 49184 | tf_op jit(solution)/shard_map/all_to_all | solution.py:75
  54.3 185.0 %while.11 = (s32[]{:T(128)}, bf16[4,128,48]{1,2,0:T(8,128)(2,1)}, bf16[4,128,48]{1,2,0:T(8,128)(2,1)S(1)}, s32[4]{0:T(128)S(1)}, s32[128]{0:T(128)S(1)}, /*index=5*/f32[4]{0:T(128)S(1)}, s32[]{:T(128)}, f32[]{:T(128)}, s32[]{:T(128)}) while((s32[]{:T(128)}, bf16[4,128,48]{1,2,0:T(8,128)(2,1)}, bf16[4,128,48]{1,2,0:T(8,128)(2,1)S(1)}, ...), condition=%wide.region_1.2_spmd, body=%wide.region_0.1_spmd.sunk | while | flops 147228448 | bytes 11572977 | solution.py:81
  54.3 0.7 dynamic_slice.21
  57.1 0.7 iota_compare_fusion.3
  57.8 35.9 %select_convert_fusion.3 = (bf16[128,5136]{1,0:T(8,128)(2,1)S(1)}, bf16[128,5136]{1,0:T(8,128)(2,1)S(1)}) fusion(f32[]{:T(128)S(6)} %div.34, s32[]{:T(128)S(6)} %select_n.52, s32[128]{0:T(128)S(1)} %get-tuple-element.172, pred[]{:T(512)S(6)} %lt.45, pred[5136]{0:T(1024)(128)(4,1)S(1)} %iota_compare_fusion.3), kind=kLoop, calls=%fused_computation.6.clone.1 | loop fusion | flops 9203712 | bytes 2635289 | tf_op jit(solution)/shard_map/convert.9
  93.7 1.3 convolution_multiply_fusion.2
  95.0 1.2 reshape.156
  96.8 0.6 pad_maximum_fusion.11
  97.7 0.8 fusion.48
  98.5 0.7 dynamic_slice.22
  100.6 0.7 dynamic_slice.21
  103.3 0.7 iota_compare_fusion.3
  104.0 35.9 %select_convert_fusion.3 = (bf16[128,5136]{1,0:T(8,128)(2,1)S(1)}, bf16[128,5136]{1,0:T(8,128)(2,1)S(1)}) fusion(f32[]{:T(128)S(6)} %div.34, s32[]{:T(128)S(6)} %select_n.52, s32[128]{0:T(128)S(1)} %get-tuple-element.172, pred[]{:T(512)S(6)} %lt.45, pred[5136]{0:T(1024)(128)(4,1)S(1)} %iota_compare_fusion.3), kind=kLoop, calls=%fused_computation.6.clone.1 | loop fusion | flops 9203712 | bytes 2635289 | tf_op jit(solution)/shard_map/convert.9
  140.0 1.3 convolution_multiply_fusion.2
  141.3 1.2 reshape.156
  143.1 0.6 pad_maximum_fusion.11
  143.9 0.8 fusion.48
  144.8 0.7 dynamic_slice.22
  146.8 0.7 dynamic_slice.21
  149.6 0.7 iota_compare_fusion.3
  150.3 35.9 %select_convert_fusion.3 = (bf16[128,5136]{1,0:T(8,128)(2,1)S(1)}, bf16[128,5136]{1,0:T(8,128)(2,1)S(1)}) fusion(f32[]{:T(128)S(6)} %div.34, s32[]{:T(128)S(6)} %select_n.52, s32[128]{0:T(128)S(1)} %get-tuple-element.172, pred[]{:T(512)S(6)} %lt.45, pred[5136]{0:T(1024)(128)(4,1)S(1)} %iota_compare_fusion.3), kind=kLoop, calls=%fused_computation.6.clone.1 | loop fusion | flops 9203712 | bytes 2635289 | tf_op jit(solution)/shard_map/convert.9
  186.2 1.3 convolution_multiply_fusion.2
  187.5 1.2 reshape.156
  189.3 0.6 pad_maximum_fusion.11
  190.2 0.8 fusion.48
  191.1 0.7 dynamic_slice.22
  193.1 0.7 dynamic_slice.21
  195.8 0.7 iota_compare_fusion.3
  196.5 35.9 %select_convert_fusion.3 = (bf16[128,5136]{1,0:T(8,128)(2,1)S(1)}, bf16[128,5136]{1,0:T(8,128)(2,1)S(1)}) fusion(f32[]{:T(128)S(6)} %div.34, s32[]{:T(128)S(6)} %select_n.52, s32[128]{0:T(128)S(1)} %get-tuple-element.172, pred[]{:T(512)S(6)} %lt.45, pred[5136]{0:T(1024)(128)(4,1)S(1)} %iota_compare_fusion.3), kind=kLoop, calls=%fused_computation.6.clone.1 | loop fusion | flops 9203712 | bytes 2635289 | tf_op jit(solution)/shard_map/convert.9
  232.5 1.3 convolution_multiply_fusion.2
  233.8 1.2 reshape.156
  235.6 0.6 pad_maximum_fusion.11
  236.4 0.8 fusion.48
  237.3 0.7 dynamic_slice.22
  239.3 1.6 copy.26
  240.9 7.5 %all-to-all-start.1 = ((bf16[128,48,4]{1,2,0:T(4,128)(2,1)}), bf16[128,48,4]{1,2,0:T(4,128)(2,1)S(1)}, u32[]{:S(2)}, u32[]{:S(2)}) async-start(bf16[128,48,4]{1,2,0:T(4,128)(2,1)} %bitcast.16), calls=%async_computation.1 | async-start | bytes 262144 | tf_op jit(solution)/shard_map/all_to_all | solution.py:83
  248.5 17.4 %all-to-all-done.1 = bf16[128,48,4]{1,2,0:T(4,128)(2,1)S(1)} async-done(((bf16[128,48,4]{1,2,0:T(4,128)(2,1)}), bf16[128,48,4]{1,2,0:T(4,128)(2,1)S(1)}, u32[]{:S(2)}, u32[]{:S(2)}) %all-to-all-start.1) | async-done | bytes 49184 | tf_op jit(solution)/shard_map/all_to_all | solution.py:83
  265.9 2.9 copy.27
  268.8 3.1 reshape.152
  272.3 1.2 convolution_bitcast_fusion
  273.7 46.3 %all-reduce.2.cloned.1.call-done = f32[32,2560]{1,0:T(8,128)} async-done(((f32[32,2560]{1,0:T(8,128)}), f32[32,2560]{1,0:T(8,128)}) %all-reduce.2.cloned.1.call-update) | async-done | bytes 327696 | tf_op jit(solution)/shard_map/psum | solution.py:96
  320.0 1.3 fusion.28
  321.4 0.7 convert_element_type.58
  (66 shorter events, 6.7 us)
Async XLA Ops:
  6.5 1.9 copy-start
  8.5 45.8 %copy-start.1 = (s32[128]{0:T(128)S(1)}, s32[128]{0:T(128)}, u32[]{:S(2)}) copy-start(s32[128]{0:T(128)} %param.14) | copy-start | bytes 1540
  8.5 45.8 %copy-start.6 = (s32[4]{0:T(128)S(1)}, s32[4]{0:T(128)}, u32[]{:S(2)}) copy-start(s32[4]{0:T(128)} %param.15) | copy-start | bytes 52
  8.5 45.8 %copy-start.7 = (f32[4]{0:T(128)S(1)}, f32[4]{0:T(128)}, u32[]{:S(2)}) copy-start(f32[4]{0:T(128)} %param.16) | copy-start | bytes 52
  11.2 42.9 %all-to-all-start = ((bf16[1,48,512]{1,0,2:T(2,128)(2,1)}), bf16[1,48,512]{1,0,2:T(2,128)(2,1)S(1)}, u32[]{:S(2)}, u32[]{:S(2)}) async-start(bf16[1,48,512]{1,0,2:T(2,128)(2,1)} %copy.24), calls=%async_computation | async-start | bytes 524288 | tf_op jit(solution)/shard_map/all_to_all | solution.py:75
  240.9 25.0 %all-to-all-start.1 = ((bf16[128,48,4]{1,2,0:T(4,128)(2,1)}), bf16[128,48,4]{1,2,0:T(4,128)(2,1)S(1)}, u32[]{:S(2)}, u32[]{:S(2)}) async-start(bf16[128,48,4]{1,2,0:T(4,128)(2,1)} %bitcast.16), calls=%async_computation.1 | async-start | bytes 262144 | tf_op jit(solution)/shard_map/all_to_all | solution.py:83
  248.4 71.5 %all-reduce.2.cloned.1.call-start = ((), (), s32[]{:S(2)}) async-start(), calls=%async_computation.2 | async-start | bytes 655360 | tf_op jit(solution)/shard_map/psum | solution.py:96
  265.9 6.0 %copy-start.4 = (bf16[1,512,1280]{2,1,0:T(8,128)(2,1)S(1)}, bf16[1,512,1280]{2,1,0:T(8,128)(2,1)}, u32[]{:S(2)}) copy-start(bf16[1,512,1280]{2,1,0:T(8,128)(2,1)} %param.13) | copy-start | bytes 3932164
  268.8 3.5 %copy-start.2 = (f32[32,8]{0,1:T(8,128)S(1)}, f32[32,8]{0,1:T(8,128)}, u32[]{:S(2)}) copy-start(f32[32,8]{0,1:T(8,128)} %param.17) | copy-start | bytes 3076
  271.9 1.6 copy-start.3
  272.2 47.8 %copy-start.5 = (f32[8,32]{1,0:T(8,128)S(1)}, f32[8,32]{1,0:T(8,128)}, u32[]{:S(2)}) copy-start(f32[8,32]{1,0:T(8,128)} %param.18) | copy-start | bytes 3076
Sparse Core Ops, SparseCore 0:
  273.6 46.3 all-reduce.1
where the time goes:
time: 331 us; the launch traced here: 329 us
  other arithmetic  152 us (46%)
  waiting for transfers between devices  86.2 us (26%)
  starting transfers between devices  27.9 us (8%)
  local copies, waits for them, and re-layouts  24.6 us (7%)
  between operations  13.6 us (4%)
  matrix products  12.8 us (4%)
  loops' own time  12 us (4%)
    another operation x8, other arithmetic  146 us
    psum x1, waiting for transfers between devices, body(): mode_values = lax.psum(partial_modes, 'lev')  46.3 us
    all_to_all x1, waiting for transfers between devices, body(): lax.all_to_all(fourier, 'lat', split_axis=2, concat_axis=0, tiled=True)  22.5 us
    all_to_all x1, starting transfers between devices, body(): lax.all_to_all(fourier, 'lat', split_axis=2, concat_axis=0, tiled=True)  20.4 us
    all_to_all x1, waiting for transfers between devices, body(): lax.all_to_all(returned, 'lat', split_axis=0, concat_axis=2, tiled=True)  17.4 us
    another operation x1, loops' own time, body(): lax.map(latitude_one, (latitudes.transpose(2, 0, 1), counts, quad_weights))  12 us
    all_to_all x1, starting transfers between devices, body(): lax.all_to_all(returned, 'lat', split_axis=0, concat_axis=2, tiled=True)  7.5 us
  transfers between devices with their start and end apart: 3, of which 3 were waited for; matrix products, arithmetic and copies ran while one was open for 0% of the time, Pallas kernels for 0%

commit v1 on v0

v1 whole, which is shorter than its diff:
```python
import functools
import math

import jax
import jax.numpy as jnp
from jax import lax
from jax.experimental import pallas as pl
from jax.experimental.pallas import tpu as pltpu
from jax.sharding import PartitionSpec as P

PTS = 5136
FIELDS = 3
XS = 4
CORES = 2
LATS = 4
LEVS = 8
LANES = 128
HALF = 64

F32 = jnp.float32
BF16 = jnp.bfloat16
MESH = pl.DeviceIdType.MESH

ROWS_BY_ROWS = (((1,), (1,)), ((), ()))


def dot(a, b):
    return jnp.dot(a, b, preferred_element_type=F32)


def dot_rows(a, b):
    return lax.dot_general(a, b, ROWS_BY_ROWS, preferred_element_type=F32)


def iota(shape, dim):
    return lax.broadcasted_iota(jnp.int32, shape, dim)


def unit(size):
    return jnp.where(iota((size, size), 0) == iota((size, size), 1), 1.0, 0.0).astype(BF16)


def half_up(value):
    return jnp.floor(value + 0.5)


def turn(steps, count, per_count):
    left = steps - half_up(steps * per_count) * count
    x = left * per_count * math.pi
    y = x * x
    s = -1.0 / 39916800
    for term in (1.0 / 362880, -1.0 / 5040, 1.0 / 120, -1.0 / 6, 1.0):
        s = s * y + term
    s = s * x
    c = 1.0 / 479001600
    for term in (-1.0 / 3628800, 1.0 / 40320, -1.0 / 720, 1.0 / 24, -0.5, 1.0):
        c = c * y + term
    return 1.0 - 2.0 * s * s, 2.0 * s * c


def kernel(
    zs, ys, spec_ref, leg_hbm, wav_row, wav_s, counts_s, weights_s, rates_s, vin_ref, vout_ref,
    out_ref,
    leg, spec2, fou, stage, wcol, table, lp, inv, out32,
    s1_out, s1_in, s2_out, s2_in, b2_out, b2_in, b1_out, b1_in, y_out, y_in, v_out, v_in,
    leg_sem, send_sem, recv_sem,
):
    ds = XS * CORES
    waves = ds * zs
    lat_all = waves * LATS
    trunc = spec_ref.shape[2]
    points = table.shape[2]
    levels_all = ys * LEVS
    me = lax.axis_index("lat")
    y = lax.axis_index("lev")
    x = me // (zs * CORES)
    z = (me // CORES) % zs
    core = me % CORES
    d = x * CORES + core

    z_peers = []
    for k in range(1, zs):
        to = (z + k) % zs
        z_peers.append((to, (x * (zs * CORES) + to * CORES + core, y)))
    d_peers = []
    for k in range(1, ds):
        to = (d + k) % ds
        d_peers.append((to, ((to // CORES) * (zs * CORES) + z * CORES + to % CORES, y)))
    y_peers = []
    for k in range(1, ys):
        to = (y + k) % ys
        y_peers.append((to, (me, to)))

    barrier = pltpu.get_barrier_semaphore()
    for _, device in z_peers + d_peers + y_peers:
        pl.semaphore_signal(barrier, inc=1, device_id=device, device_id_type=MESH)

    def send(number, source, arrive, slot, peers):
        pltpu.make_async_copy(source(slot), arrive.at[slot], recv_sem.at[number]).start()
        for to, device in peers:
            pltpu.make_async_remote_copy(
                src_ref=source(to), dst_ref=arrive.at[slot],
                send_sem=send_sem.at[number], recv_sem=recv_sem.at[number],
                device_id=device, device_id_type=MESH,
            ).start()

    def arrived(number, arrive):
        pltpu.make_async_copy(arrive, arrive, recv_sem.at[number]).wait()

    def sent(number, arrive, count):
        part = arrive.at[pl.ds(0, count)]
        pltpu.make_async_copy(part, part, send_sem.at[number]).wait()

    part_rows = lat_all // XS
    loads = []
    for k in range(XS):
        rows = pl.ds(k * part_rows, part_rows)
        loads.append(pltpu.make_async_copy(leg_hbm.at[0, rows], leg.at[rows], leg_sem.at[k]))
        loads[-1].start()

    order = wav_s[me]
    kept = iota((1, trunc), 1) >= order
    columns = spec_ref.shape[1]
    masked = jnp.where(kept, spec_ref[0].astype(F32), 0.0).astype(BF16)
    blank = jnp.zeros((HALF - columns, trunc), BF16)
    spec2[0:columns] = masked
    spec2[columns:HALF] = blank
    spec2[HALF : HALF + columns] = masked
    spec2[HALF + columns :] = blank

    lane = iota((levels_all, 4 * levels_all), 1) % levels_all
    spread = jnp.zeros((levels_all, 4 * levels_all), F32)
    for k in range(LEVS):
        spread = jnp.where(lane == y * LEVS + k, vin_ref[:, k : k + 1], spread)
    v_out[...] = spread

    for k in range(XS):
        loads[k].wait()
        rows = pl.ds(k * part_rows, part_rows)
        fou[rows] = dot_rows(leg[rows], spec2[...])

    first_half = iota((LATS, LANES), 1) < HALF
    for to in range(zs):
        for k in range(XS):
            low = fou[pl.ds(k * part_rows + 8 * to, 4, stride=2)]
            high = fou[pl.ds(k * part_rows + 8 * to + 1, 4, stride=2)]
            stage[pl.ds(to * 4 * XS + 4 * k, 4)] = jnp.where(first_half, low, high)
    s1_out[...] = stage[...].astype(BF16).reshape(s1_out.shape)

    pl.semaphore_wait(barrier, len(z_peers) + len(d_peers) + len(y_peers))
    send(0, lambda slot: s1_out.at[slot], s1_in, z, z_peers)
    send(5, lambda slot: v_out, v_in, y, y_peers)

    place = iota((waves, waves), 0)
    across = iota((waves, waves), 1)
    natural = (place // (CORES * zs)) * (CORES * zs) + (place % zs) * CORES + (place // zs) % CORES
    waves_f = wav_row[...].astype(F32)
    column = jnp.sum(jnp.where(across == natural, waves_f, 0.0), axis=1, keepdims=True)
    row = jnp.sum(jnp.where(across == place, column, 0.0), axis=0, keepdims=True)
    even = row - 2.0 * jnp.floor(row * 0.5) == 0.0
    parity = jnp.where(even, 1.0, -1.0)
    wcol[...] = jnp.broadcast_to(column, wcol.shape)

    chunk = waves // 4

    def table_part(step, carry):
        lat = step // 4
        begin = pl.multiple_of((step % 4) * chunk, chunk)
        count = jnp.full((chunk, LANES), counts_s[lat].astype(F32), F32)
        per_count = 1.0 / count
        waves_here = wcol[pl.ds(begin, chunk)]
        offset = iota((chunk, LANES), 1).astype(F32)
        c, s = turn(waves_here * offset, count, per_count)
        step_c, step_s = turn(waves_here * float(LANES), count, per_count)
        for a in range(points // LANES):
            at = slice(a * LANES, (a + 1) * LANES)
            table[lat, pl.ds(begin, chunk), at] = c.astype(BF16)
            table[lat, pl.ds(waves + begin, chunk), at] = s.astype(BF16)
            c, s = c * step_c - s * step_s, s * step_c + c * step_s
        return carry

    lax.fori_loop(0, LATS * 4, table_part, 0)

    arrived(0, s1_in)
    stage[...] = s1_in[...].astype(F32).reshape(stage.shape)
    slots = 4 * XS
    first_half = iota((zs, LANES), 1) < HALF
    for k in range(ds):
        for t in range(2):
            s2_out[k, t] = stage[pl.ds(2 * k + t, zs, stride=slots)].astype(BF16)
    send(1, lambda slot: s2_out.at[slot], s2_in, d, d_peers)

    degree = iota((1, trunc), 1).astype(F32)
    growth = degree * (degree + 1.0) / float(trunc * trunc)
    at_mode = iota((levels_all, LANES), 0)
    rates = jnp.zeros((levels_all, LANES), F32)
    for k in range(levels_all):
        rates = jnp.where(at_mode == k, rates_s[k], rates)
    inv[...] = 1.0 / (1.0 + rates[:, 0:1] * growth)

    r = iota((LANES, LANES), 0)
    field = (r // LEVS) % 4
    wanted = (r // HALF) * HALF + (r % LEVS) * 6 + 2 * field + (r // 32) % 2
    pick = jnp.where((iota((LANES, LANES), 1) == wanted) & (field < 3), 1.0, 0.0).astype(BF16)

    arrived(1, s2_in)

    def grid_pair(t, carry):
        got = s2_in[:, t].reshape(waves, LANES)
        coeffs = dot_rows(pick, got)
        blocks = []
        for low in range(2):
            lat = 2 * t + low
            cosine = coeffs[low * HALF : low * HALF + 24]
            sine = coeffs[low * HALF + 32 : low * HALF + 56]
            turned = parity * cosine
            turned_sine = parity * sine
            w = jnp.concatenate(
                [
                    jnp.concatenate([cosine, sine], 1),
                    jnp.concatenate([cosine, -sine], 1),
                    jnp.concatenate([turned, turned_sine], 1),
                    jnp.concatenate([turned, -turned_sine], 1),
                ],
                0,
            ).astype(BF16)
            grid = dot(w, table[lat]) * (1.0 / math.sqrt(2 * waves))
            count = counts_s[lat]
            quarter = count // 4
            j = iota((1, points), 1)
            share = jnp.where((j == 0) | (j == quarter), 0.5, 1.0)
            share = jnp.where(j > quarter, 0.0, share)
            tend = []
            for q in range(4):
                g = [grid[q * 24 + f * 8 : q * 24 + f * 8 + 8] for f in range(FIELDS)]
                tend.append([g[0] - g[1] * g[2], g[1] + g[0] * g[2], g[2] - g[0] * g[1]])
            folded = [[], [], [], []]
            for f in range(FIELDS):
                t0, t1, t2, t3 = (tend[q][f] * share for q in range(4))
                plus, minus = t0 + t1, t0 - t1
                plus_far, minus_far = t2 + t3, t2 - t3
                folded[0].append(plus + plus_far)
                folded[1].append(plus - plus_far)
                folded[2].append(minus + minus_far)
                folded[3].append(minus - minus_far)
            u = jnp.concatenate(folded[0] + folded[1] + folded[2] + folded[3], 0).astype(BF16)
            back = dot_rows(u, table[lat])
            count_f = jnp.full((1, waves), count.astype(F32), F32)
            factor = jnp.full((1, waves), weights_s[lat], F32) / jnp.sqrt(count_f)
            cos_out = jnp.where(even, back[0:24, :waves], back[24:48, :waves]) * factor
            sin_out = jnp.where(even, back[48:72, waves:], back[72:96, waves:]) * -factor
            for f in range(FIELDS):
                blocks.append(cos_out[f * 8 : f * 8 + 8])
                blocks.append(sin_out[f * 8 : f * 8 + 8])
            blocks.append(jnp.zeros((16, waves), F32))
        returned = jnp.concatenate(blocks, 0).astype(BF16)
        b2_out[:, t] = dot_rows(unit(waves), returned).astype(BF16).reshape(ds, zs, LANES)
        return carry

    lax.fori_loop(0, 2, grid_pair, 0)
    send(2, lambda slot: b2_out.at[slot], b2_in, d, d_peers)

    target = iota((1, lat_all), 1)
    spot = ((target // 8) % zs) * slots + (target // part_rows) * 4 + (target // 2) % 4
    line = iota((lat_all // 2, lat_all), 0)
    for low in range(2):
        pick_rows = jnp.where((spot == line) & (target % 2 == low), 1.0, 0.0).astype(BF16)
        lp[low] = dot(pick_rows, leg[...]).astype(BF16)

    arrived(2, b2_in)
    stage[...] = b2_in[...].astype(F32).reshape(stage.shape)
    for to in range(zs):
        b1_out[to] = stage[pl.ds(to, slots, stride=zs)].astype(BF16)
    send(3, lambda slot: b1_out.at[slot], b1_in, z, z_peers)

    arrived(5, v_in)
    lane = iota((levels_all, 4 * levels_all), 1)
    whole = v_in[0]
    for k in range(1, ys):
        whole = whole + v_in[k]
    whole_high = whole.astype(BF16).astype(F32)
    into = jnp.where(lane < 2 * levels_all, whole_high, whole - whole_high).astype(BF16)
    lane = iota((LEVS, 4 * levels_all), 1)
    whole = jnp.zeros((LEVS, 4 * levels_all), F32)
    for k in range(levels_all):
        whole = jnp.where(lane % levels_all == k, vout_ref[:, k : k + 1], whole)
    whole_high = whole.astype(BF16).astype(F32)
    onto = jnp.where(lane < 2 * levels_all, whole_high, whole - whole_high).astype(BF16)

    def place_rows(begin, value):
        for a in range(trunc // LANES):
            out32[a, pl.ds(begin, LEVS, stride=6)] = value[:, a * LANES : (a + 1) * LANES]

    def high_low(value):
        high = value.astype(BF16)
        low = (value - high.astype(F32)).astype(BF16)
        return jnp.concatenate([high, low, high, low], 0)

    arrived(3, b1_in)
    back = dot_rows(unit(LANES), b1_in[...].reshape(lat_all // 2, LANES)).astype(BF16)
    y_out[0] = back[0:16]
    y_out[1] = back[HALF : HALF + 16]
    send(4, lambda slot: y_out, y_in, y, y_peers)
    others = dot(back[16:48], lp[0]) + dot(back[HALF + 16 : HALF + 48], lp[1])
    others = jnp.where(kept, others, 0.0)
    for f in (1, 2):
        for part in range(2):
            begin = (f - 1) * 16 + part * 8
            place_rows(2 * f + part, others[begin : begin + LEVS])

    arrived(4, y_in)
    first = y_in[:, 0].reshape(ys * 16, lat_all // 2)
    second = y_in[:, 1].reshape(ys * 16, lat_all // 2)
    diverg = dot(first, lp[0]) + dot(second, lp[1])
    diverg = jnp.where(kept, diverg, 0.0)
    for part in range(2):
        of_part = [diverg[k * 16 + part * 8 : k * 16 + part * 8 + 8] for k in range(ys)]
        modes = dot(into, high_low(jnp.concatenate(of_part, 0)))
        solved = dot(onto, high_low(modes * inv[...]))
        place_rows(part, solved)
    for a in range(trunc // LANES):
        out_ref[0, :, a * LANES : (a + 1) * LANES] = out32[a].astype(BF16)

    sent(0, s1_in, zs - 1)
    sent(1, s2_in, ds - 1)
    sent(2, b2_in, ds - 1)
    sent(3, b1_in, zs - 1)
    sent(4, y_in, ys - 1)
    sent(5, v_in, ys - 1)


def body(spec_in, legendre, wavenum, counts, quad_weights, vert_in, vert_out, mode_rates, zs, ys):
    _, columns, trunc = spec_in.shape
    ds = XS * CORES
    waves = ds * zs
    lat_all = waves * LATS
    levels_all = ys * LEVS
    points = -(-(PTS // 4 + 1) // LANES) * LANES
    vmem = pl.BlockSpec(memory_space=pltpu.VMEM)
    smem = pl.BlockSpec(memory_space=pltpu.SMEM)
    by_z = (zs, 4 * XS, LANES)
    by_d = (ds, 2, zs, LANES)
    return pl.pallas_call(
        functools.partial(kernel, zs, ys),
        out_shape=jax.ShapeDtypeStruct((1, columns, trunc), BF16),
        in_specs=[vmem, pl.BlockSpec(memory_space=pl.ANY), vmem, smem, smem, smem, smem, vmem, vmem],
        out_specs=vmem,
        scratch_shapes=[
            pltpu.VMEM((lat_all, trunc), BF16),
            pltpu.VMEM((LANES, trunc), BF16),
            pltpu.VMEM((lat_all, LANES), F32),
            pltpu.VMEM((lat_all // 2, LANES), F32),
            pltpu.VMEM((waves, LANES), F32),
            pltpu.VMEM((LATS, 2 * waves, points), BF16),
            pltpu.VMEM((2, lat_all // 2, trunc), BF16),
            pltpu.VMEM((levels_all, trunc), F32),
            pltpu.VMEM((trunc // LANES, columns, LANES), F32),
            pltpu.VMEM(by_z, BF16),
            pltpu.VMEM(by_z, BF16),
            pltpu.VMEM(by_d, BF16),
            pltpu.VMEM(by_d, BF16),
            pltpu.VMEM(by_d, BF16),
            pltpu.VMEM(by_d, BF16),
            pltpu.VMEM(by_z, BF16),
            pltpu.VMEM(by_z, BF16),
            pltpu.VMEM((2, 16, lat_all // 2), BF16),
            pltpu.VMEM((ys, 2, 16, lat_all // 2), BF16),
            pltpu.VMEM((levels_all, 4 * levels_all), F32),
            pltpu.VMEM((ys, levels_all, 4 * levels_all), F32),
            pltpu.SemaphoreType.DMA((XS,)),
            pltpu.SemaphoreType.DMA((6,)),
            pltpu.SemaphoreType.DMA((6,)),
        ],
        compiler_params=pltpu.CompilerParams(
            collective_id=0, has_side_effects=True, vmem_limit_bytes=48 * 1024 * 1024
        ),
    )(
        spec_in, legendre, wavenum.reshape(1, -1), wavenum, counts, quad_weights, mode_rates,
        vert_in, vert_out,
    )


def solution(mesh):
    zs = mesh.shape["lat"] // (XS * CORES)
    return jax.shard_map(
        functools.partial(body, zs=zs, ys=mesh.shape["lev"]),
        mesh=mesh,
        in_specs=(
            P("lat", "lev", None),
            P("lat", None, None),
            P(),
            P("lat"),
            P("lat"),
            P(None, "lev"),
            P("lev", None),
            P(),
        ),
        out_specs=P("lat", "lev", None),
        check_vma=False,
    )
```

time: 331 us -> 55.9 us (0.17)
  other arithmetic: 152 us -> 0 us
  waiting for transfers between devices: 86.2 us -> 0 us
  Pallas kernels: 0 us -> 48.7 us
  starting transfers between devices: 27.9 us -> 0 us
  local copies, waits for them, and re-layouts: 24.6 us -> 6.93 us
  between operations: 13.6 us -> 0.02 us
  matrix products: 12.8 us -> 0 us
  loops' own time: 12 us -> 0 us
    another operation x20 -> x0, other arithmetic: 148 us -> none
    pallas_call x0 -> x1, Pallas kernels: none -> 48.7 us  [body(): pl.pallas_call(functools.partial(kernel, zs, ys), out_shape=jax.ShapeDtyp...]
    psum x1 -> x0, waiting for transfers between devices: 46.3 us -> none  [body(): mode_values = lax.psum(partial_modes, 'lev')]
    all_to_all x2 -> x0, waiting for transfers between devices: 39.9 us -> none  [the longest x1 22.5 us: body(): lax.all_to_all(fourier, 'lat', split_axis=2, concat_axis=0, tiled=True)]
    all_to_all x2 -> x0, starting transfers between devices: 27.9 us -> none  [the longest x1 20.4 us: body(): lax.all_to_all(fourier, 'lat', split_axis=2, concat_axis=0, tiled=True)]
    dot_general x12 -> x0, matrix products: 12.8 us -> none  [the longest x4 5.08 us: grid_step(): lax.dot_general(stacked, trig_table, (((0,), (0,)), ((), ())), preferred_...]
    another operation x1 -> x0, loops' own time: 12 us -> none  [body(): lax.map(latitude_one, (latitudes.transpose(2, 0, 1), counts, quad_weights))]
    unnamed x18 -> x16, local copies, waits for them, and re-layouts: 0.09 us -> 6.93 us
  transfers between devices with their start and end apart: 3 -> 0, of which waited for: 3 -> 0; matrix products, arithmetic and copies ran while one was open for 0% -> 0% of each run, Pallas kernels for 0% -> 0%
where the time goes in v1:
time: 55.9 us; the launch traced here: 55.7 us
  Pallas kernels  48.7 us (87%)
  local copies, waits for them, and re-layouts  6.93 us (12%)
    pallas_call x1, Pallas kernels, body(): pl.pallas_call(functools.partial(kernel, zs, ys), out_shape=jax.ShapeDtyp...  48.7 us
    unnamed x16, local copies, waits for them, and re-layouts  6.93 us

profile of v1, /device:TPU:1, one launch (start us, length us, event | category | flops | bytes accessed | tf_op | source)
XLA Modules:
  0.0 55.7 jit_solution(6168018798315508480)
XLA Ops:
  0.0 0.8 %copy.9.vin_ref = f32[32,8]{1,0:T(8,128)S(1)} copy(f32[32,8]{0,1:T(8,128)} %param.13) | data formatting | bytes 2048 | tf_op args[5]
  0.8 0.0 copy-start
  0.8 1.3 %copy-done = bf16[1,512,1280]{2,1,0:T(8,128)(2,1)S(1)} copy-done((bf16[1,512,1280]{2,1,0:T(8,128)(2,1)S(1)}, bf16[1,512,1280]{2,1,0:T(8,128)(2,1)}, u32[]{:S(2)}) %copy-start) | copy-done | bytes 1310744
  2.1 0.0 copy-start.1
  2.1 0.9 %copy-done.1 = bf16[1,48,1280]{2,1,0:T(8,128)(2,1)S(1)} copy-done((bf16[1,48,1280]{2,1,0:T(8,128)(2,1)S(1)}, bf16[1,48,1280]{2,1,0:T(8,128)(2,1)}, u32[]{:S(2)}) %copy-start.1) | copy-done | bytes 122904
  3.0 0.0 copy-start.2
  3.0 0.7 %copy-done.2 = f32[8,32]{1,0:T(8,128)S(1)} copy-done((f32[8,32]{1,0:T(8,128)S(1)}, f32[8,32]{1,0:T(8,128)}, u32[]{:S(2)}) %copy-start.2) | copy-done | bytes 1048
  3.7 0.0 copy-start.3
  3.7 0.7 %copy-done.3 = s32[128]{0:T(128)S(1)} copy-done((s32[128]{0:T(128)S(1)}, s32[128]{0:T(128)}, u32[]{:S(2)}) %copy-start.3) | copy-done | bytes 536
  4.3 0.0 copy-start.4
  4.3 0.7 %copy-done.4 = s32[4]{0:T(128)S(1)} copy-done((s32[4]{0:T(128)S(1)}, s32[4]{0:T(128)}, u32[]{:S(2)}) %copy-start.4) | copy-done | bytes 40
  5.0 0.0 copy-start.5
  5.0 0.7 %copy-done.5 = f32[4]{0:T(128)S(1)} copy-done((f32[4]{0:T(128)S(1)}, f32[4]{0:T(128)}, u32[]{:S(2)}) %copy-start.5) | copy-done | bytes 40
  5.6 0.0 copy-start.6
  5.6 0.7 %copy-done.6 = f32[32]{0:T(128)S(1)} copy-done((f32[32]{0:T(128)S(1)}, f32[32]{0:T(128)}, u32[]{:S(2)}) %copy-start.6) | copy-done | bytes 152
  6.3 48.7 %shard_map.82 = bf16[1,48,1280]{2,1,0:T(8,128)(2,1)S(1)} custom-call(bf16[1,48,1280]{2,1,0:T(8,128)(2,1)S(1)} %copy-done.1, bf16[1,512,1280]{2,1,0:T(8,128)(2,1)S(1)} %copy-done, s32[1,128]{1,0:T(1,128)S(1)} %bitcast.1, s32[128]{0:T(128)S(1)} %copy-done.3, s32[4]{0:T(128)S(1)} %copy-done.4, f32[4]{0:T(128)S(1)} %copy-done.5, f32[32]{0:T(128)S(1)} %copy-done.6, ...), custom_call_target="tpu_custom_call" | custom-call | tf_op jit(solution)/shard_map/pallas_call | solution.py:343
  55.0 0.7 %copy.11 = bf16[1,48,1280]{2,1,0:T(8,128)(2,1)} copy(bf16[1,48,1280]{2,1,0:T(8,128)(2,1)S(1)} %shard_map.82) | data formatting | bytes 245760
Async XLA Ops:
  0.8 1.3 %copy-start = (bf16[1,512,1280]{2,1,0:T(8,128)(2,1)S(1)}, bf16[1,512,1280]{2,1,0:T(8,128)(2,1)}, u32[]{:S(2)}) copy-start(bf16[1,512,1280]{2,1,0:T(8,128)(2,1)} %leg_hbm.1) | copy-start | bytes 3932164
  2.1 0.9 %copy-start.1 = (bf16[1,48,1280]{2,1,0:T(8,128)(2,1)S(1)}, bf16[1,48,1280]{2,1,0:T(8,128)(2,1)}, u32[]{:S(2)}) copy-start(bf16[1,48,1280]{2,1,0:T(8,128)(2,1)} %spec_ref.1) | copy-start | bytes 368644
  3.0 0.7 %copy-start.2 = (f32[8,32]{1,0:T(8,128)S(1)}, f32[8,32]{1,0:T(8,128)}, u32[]{:S(2)}) copy-start(f32[8,32]{1,0:T(8,128)} %vout_ref.1) | copy-start | bytes 3076
  3.7 0.7 %copy-start.3 = (s32[128]{0:T(128)S(1)}, s32[128]{0:T(128)}, u32[]{:S(2)}) copy-start(s32[128]{0:T(128)} %wav_s.1) | copy-start | bytes 1540
  4.3 0.7 %copy-start.4 = (s32[4]{0:T(128)S(1)}, s32[4]{0:T(128)}, u32[]{:S(2)}) copy-start(s32[4]{0:T(128)} %counts_s.1) | copy-start | bytes 52
  5.0 0.7 %copy-start.5 = (f32[4]{0:T(128)S(1)}, f32[4]{0:T(128)}, u32[]{:S(2)}) copy-start(f32[4]{0:T(128)} %weights_s.1) | copy-start | bytes 52
  5.6 0.7 %copy-start.6 = (f32[32]{0:T(128)S(1)}, f32[32]{0:T(128)}, u32[]{:S(2)}) copy-start(f32[32]{0:T(128)} %rates_s.1) | copy-start | bytes 388

commit v2 on v1

--- a/solution.py
+++ b/solution.py
@@ -59,16 +59,17 @@
 
 
 def kernel(
-    zs, ys, spec_ref, leg_hbm, wav_row, wav_s, counts_s, weights_s, rates_s, vin_ref, vout_ref,
+    zs, ys, spec_hbm, leg_hbm, wav_hbm, wav_row_hbm, counts_hbm, weights_hbm, rates_hbm, vin_hbm, vout_hbm,
     out_ref,
+    spec_ref, wav_row, vin_ref, vout_ref, wav_s, counts_s, weights_s, rates_s,
     leg, spec2, fou, stage, wcol, table, lp, inv, out32,
-    s1_out, s1_in, s2_out, s2_in, b2_out, b2_in, b1_out, b1_in, y_out, y_in, v_out, v_in,
-    leg_sem, send_sem, recv_sem,
+    s1_out, s1_in, s2_out, s2_in, b_out, b_in, y_out, y_in, v_out, v_in,
+    load_sem, leg_sem, send_sem, recv_sem,
 ):
     ds = XS * CORES
     waves = ds * zs
     lat_all = waves * LATS
-    trunc = spec_ref.shape[2]
+    trunc = spec_ref.shape[1]
     points = table.shape[2]
     levels_all = ys * LEVS
     me = lax.axis_index("lat")
@@ -78,30 +79,50 @@
     core = me % CORES
     d = x * CORES + core
 
+    def device(to_x, to_z, to_core):
+        return (to_x * (zs * CORES) + to_z * CORES + to_core, y)
+
     z_peers = []
-    for k in range(1, zs):
-        to = (z + k) % zs
-        z_peers.append((to, (x * (zs * CORES) + to * CORES + core, y)))
+    for i in range(zs - 1):
+        away = zs // 2 - (i + 1) // 2 if i % 2 else zs // 2 + i // 2
+        to = (z + away) % zs
+        z_peers.append((to, device(x, to, core)))
+    d_away = [(k, c) for k in sorted(range(XS), key=lambda k: -min(k, XS - k)) for c in range(CORES)]
     d_peers = []
-    for k in range(1, ds):
-        to = (d + k) % ds
-        d_peers.append((to, ((to // CORES) * (zs * CORES) + z * CORES + to % CORES, y)))
+    for k, c in d_away:
+        to_x, to_core = (x + k) % XS, (core + c) % CORES
+        if (k, c) != (0, 0):
+            d_peers.append((to_x * CORES + to_core, device(to_x, z, to_core)))
     y_peers = []
     for k in range(1, ys):
         to = (y + k) % ys
         y_peers.append((to, (me, to)))
 
     barrier = pltpu.get_barrier_semaphore()
-    for _, device in z_peers + d_peers + y_peers:
-        pl.semaphore_signal(barrier, inc=1, device_id=device, device_id_type=MESH)
+    for _, to in z_peers + d_peers + y_peers:
+        pl.semaphore_signal(barrier, inc=1, device_id=to, device_id_type=MESH)
+
+    loads = []
+    for source, target in (
+        (spec_hbm.at[0], spec_ref), (wav_hbm, wav_s), (counts_hbm, counts_s), (weights_hbm, weights_s),
+        (rates_hbm, rates_s), (wav_row_hbm, wav_row), (vin_hbm, vin_ref), (vout_hbm, vout_ref),
+    ):
+        loads.append(pltpu.make_async_copy(source, target, load_sem.at[len(loads)]))
+        loads[-1].start()
+    part_rows = lat_all // XS
+    leg_loads = []
+    for k in range(XS):
+        rows = pl.ds(k * part_rows, part_rows)
+        leg_loads.append(pltpu.make_async_copy(leg_hbm.at[0, rows], leg.at[rows], leg_sem.at[k]))
+        leg_loads[-1].start()
 
     def send(number, source, arrive, slot, peers):
         pltpu.make_async_copy(source(slot), arrive.at[slot], recv_sem.at[number]).start()
-        for to, device in peers:
+        for to, to_device in peers:
             pltpu.make_async_remote_copy(
                 src_ref=source(to), dst_ref=arrive.at[slot],
                 send_sem=send_sem.at[number], recv_sem=recv_sem.at[number],
-                device_id=device, device_id_type=MESH,
+                device_id=to_device, device_id_type=MESH,
             ).start()
 
     def arrived(number, arrive):
@@ -111,31 +132,20 @@
         part = arrive.at[pl.ds(0, count)]
         pltpu.make_async_copy(part, part, send_sem.at[number]).wait()
 
-    part_rows = lat_all // XS
-    loads = []
-    for k in range(XS):
-        rows = pl.ds(k * part_rows, part_rows)
-        loads.append(pltpu.make_async_copy(leg_hbm.at[0, rows], leg.at[rows], leg_sem.at[k]))
-        loads[-1].start()
-
+    loads[0].wait()
+    loads[1].wait()
     order = wav_s[me]
     kept = iota((1, trunc), 1) >= order
-    columns = spec_ref.shape[1]
-    masked = jnp.where(kept, spec_ref[0].astype(F32), 0.0).astype(BF16)
+    columns = spec_ref.shape[0]
+    masked = jnp.where(kept, spec_ref[...].astype(F32), 0.0).astype(BF16)
     blank = jnp.zeros((HALF - columns, trunc), BF16)
     spec2[0:columns] = masked
     spec2[columns:HALF] = blank
     spec2[HALF : HALF + columns] = masked
     spec2[HALF + columns :] = blank
 
-    lane = iota((levels_all, 4 * levels_all), 1) % levels_all
-    spread = jnp.zeros((levels_all, 4 * levels_all), F32)
-    for k in range(LEVS):
-        spread = jnp.where(lane == y * LEVS + k, vin_ref[:, k : k + 1], spread)
-    v_out[...] = spread
-
     for k in range(XS):
-        loads[k].wait()
+        leg_loads[k].wait()
         rows = pl.ds(k * part_rows, part_rows)
         fou[rows] = dot_rows(leg[rows], spec2[...])
 
@@ -149,7 +159,13 @@
 
     pl.semaphore_wait(barrier, len(z_peers) + len(d_peers) + len(y_peers))
     send(0, lambda slot: s1_out.at[slot], s1_in, z, z_peers)
-    send(5, lambda slot: v_out, v_in, y, y_peers)
+
+    for load in loads[2:]:
+        load.wait()
+
+    v_out[...] = jnp.zeros(v_out.shape, F32)
+    v_out[:, 0:levels_all] = vin_ref[...]
+    send(4, lambda slot: v_out, v_in, y, y_peers)
 
     place = iota((waves, waves), 0)
     across = iota((waves, waves), 1)
@@ -190,14 +206,6 @@
             s2_out[k, t] = stage[pl.ds(2 * k + t, zs, stride=slots)].astype(BF16)
     send(1, lambda slot: s2_out.at[slot], s2_in, d, d_peers)
 
-    degree = iota((1, trunc), 1).astype(F32)
-    growth = degree * (degree + 1.0) / float(trunc * trunc)
-    at_mode = iota((levels_all, LANES), 0)
-    rates = jnp.zeros((levels_all, LANES), F32)
-    for k in range(levels_all):
-        rates = jnp.where(at_mode == k, rates_s[k], rates)
-    inv[...] = 1.0 / (1.0 + rates[:, 0:1] * growth)
-
     r = iota((LANES, LANES), 0)
     field = (r // LEVS) % 4
     wanted = (r // HALF) * HALF + (r % LEVS) * 6 + 2 * field + (r // 32) % 2
@@ -205,7 +213,7 @@
 
     arrived(1, s2_in)
 
-    def grid_pair(t, carry):
+    def grid_pair(t):
         got = s2_in[:, t].reshape(waves, LANES)
         coeffs = dot_rows(pick, got)
         blocks = []
@@ -254,32 +262,50 @@
                 blocks.append(sin_out[f * 8 : f * 8 + 8])
             blocks.append(jnp.zeros((16, waves), F32))
         returned = jnp.concatenate(blocks, 0).astype(BF16)
-        b2_out[:, t] = dot_rows(unit(waves), returned).astype(BF16).reshape(ds, zs, LANES)
+        stage[pl.ds(t, waves, stride=2)] = dot_rows(unit(waves), returned)
+
+    for t in range(2):
+        grid_pair(t)
+    b_out[...] = stage[...].astype(BF16).reshape(b_out.shape)
+    def send_back(away, pairs):
+        to_z = (z + away) % zs
+        for k, c in pairs:
+            to_x, to_core = (x + k) % XS, (core + c) % CORES
+            pltpu.make_async_remote_copy(
+                src_ref=b_out.at[(to_x * CORES + to_core) * zs + to_z], dst_ref=b_in.at[me],
+                send_sem=send_sem.at[2], recv_sem=recv_sem.at[2],
+                device_id=device(to_x, to_z, to_core), device_id_type=MESH,
+            ).start()
+
+    def send_ring(i, carry):
+        odd = i % 2
+        send_back(odd * (zs // 2 - (i + 1) // 2) + (1 - odd) * (zs // 2 + i // 2), d_away)
         return carry
 
-    lax.fori_loop(0, 2, grid_pair, 0)
-    send(2, lambda slot: b2_out.at[slot], b2_in, d, d_peers)
+    lax.fori_loop(0, zs - 1, send_ring, 0)
+    send_back(0, [pair for pair in d_away if pair != (0, 0)])
+    pltpu.make_async_copy(b_out.at[d * zs + z], b_in.at[me], recv_sem.at[2]).start()
 
     target = iota((1, lat_all), 1)
-    spot = ((target // 8) % zs) * slots + (target // part_rows) * 4 + (target // 2) % 4
     line = iota((lat_all // 2, lat_all), 0)
     for low in range(2):
-        pick_rows = jnp.where((spot == line) & (target % 2 == low), 1.0, 0.0).astype(BF16)
+        pick_rows = jnp.where(target == 2 * line + low, 1.0, 0.0).astype(BF16)
         lp[low] = dot(pick_rows, leg[...]).astype(BF16)
 
-    arrived(2, b2_in)
-    stage[...] = b2_in[...].astype(F32).reshape(stage.shape)
-    for to in range(zs):
-        b1_out[to] = stage[pl.ds(to, slots, stride=zs)].astype(BF16)
-    send(3, lambda slot: b1_out.at[slot], b1_in, z, z_peers)
-
-    arrived(5, v_in)
-    lane = iota((levels_all, 4 * levels_all), 1)
-    whole = v_in[0]
-    for k in range(1, ys):
-        whole = whole + v_in[k]
+    degree = iota((1, trunc), 1).astype(F32)
+    growth = degree * (degree + 1.0) / float(trunc * trunc)
+    at_mode = iota((levels_all, LANES), 0)
+    rates = jnp.zeros((levels_all, LANES), F32)
+    for k in range(levels_all):
+        rates = jnp.where(at_mode == k, rates_s[k], rates)
+    inv[...] = 1.0 / (1.0 + rates[:, 0:1] * growth)
+
+    arrived(4, v_in)
+    whole = v_in[...].reshape(levels_all, LANES)
     whole_high = whole.astype(BF16).astype(F32)
-    into = jnp.where(lane < 2 * levels_all, whole_high, whole - whole_high).astype(BF16)
+    whole_low = whole - whole_high
+    into = jnp.concatenate([whole_high, whole_high, whole_low, whole_low], 0).astype(BF16)
+    into = dot_rows(unit(LANES), into)[0:levels_all].astype(BF16)
     lane = iota((LEVS, 4 * levels_all), 1)
     whole = jnp.zeros((LEVS, 4 * levels_all), F32)
     for k in range(levels_all):
@@ -296,11 +322,11 @@
         low = (value - high.astype(F32)).astype(BF16)
         return jnp.concatenate([high, low, high, low], 0)
 
-    arrived(3, b1_in)
-    back = dot_rows(unit(LANES), b1_in[...].reshape(lat_all // 2, LANES)).astype(BF16)
+    arrived(2, b_in)
+    back = dot_rows(unit(LANES), b_in[...].reshape(lat_all // 2, LANES)).astype(BF16)
     y_out[0] = back[0:16]
     y_out[1] = back[HALF : HALF + 16]
-    send(4, lambda slot: y_out, y_in, y, y_peers)
+    send(3, lambda slot: y_out, y_in, y, y_peers)
     others = dot(back[16:48], lp[0]) + dot(back[HALF + 16 : HALF + 48], lp[1])
     others = jnp.where(kept, others, 0.0)
     for f in (1, 2):
@@ -308,7 +334,7 @@
             begin = (f - 1) * 16 + part * 8
             place_rows(2 * f + part, others[begin : begin + LEVS])
 
-    arrived(4, y_in)
+    arrived(3, y_in)
     first = y_in[:, 0].reshape(ys * 16, lat_all // 2)
     second = y_in[:, 1].reshape(ys * 16, lat_all // 2)
     diverg = dot(first, lp[0]) + dot(second, lp[1])
@@ -323,10 +349,9 @@
 
     sent(0, s1_in, zs - 1)
     sent(1, s2_in, ds - 1)
-    sent(2, b2_in, ds - 1)
-    sent(3, b1_in, zs - 1)
-    sent(4, y_in, ys - 1)
-    sent(5, v_in, ys - 1)
+    sent(2, b_in, waves - 1)
+    sent(3, y_in, ys - 1)
+    sent(4, v_in, ys - 1)
 
 
 def body(spec_in, legendre, wavenum, counts, quad_weights, vert_in, vert_out, mode_rates, zs, ys):
@@ -336,16 +361,23 @@
     lat_all = waves * LATS
     levels_all = ys * LEVS
     points = -(-(PTS // 4 + 1) // LANES) * LANES
-    vmem = pl.BlockSpec(memory_space=pltpu.VMEM)
-    smem = pl.BlockSpec(memory_space=pltpu.SMEM)
+    any_place = pl.BlockSpec(memory_space=pl.ANY)
     by_z = (zs, 4 * XS, LANES)
     by_d = (ds, 2, zs, LANES)
     return pl.pallas_call(
         functools.partial(kernel, zs, ys),
         out_shape=jax.ShapeDtypeStruct((1, columns, trunc), BF16),
-        in_specs=[vmem, pl.BlockSpec(memory_space=pl.ANY), vmem, smem, smem, smem, smem, vmem, vmem],
-        out_specs=vmem,
+        in_specs=[any_place] * 9,
+        out_specs=pl.BlockSpec(memory_space=pltpu.VMEM),
         scratch_shapes=[
+            pltpu.VMEM((columns, trunc), BF16),
+            pltpu.VMEM((1, waves), jnp.int32),
+            pltpu.VMEM((LEVS, levels_all), F32),
+            pltpu.VMEM((LEVS, levels_all), F32),
+            pltpu.SMEM((waves,), jnp.int32),
+            pltpu.SMEM((LATS,), jnp.int32),
+            pltpu.SMEM((LATS,), F32),
+            pltpu.SMEM((levels_all,), F32),
             pltpu.VMEM((lat_all, trunc), BF16),
             pltpu.VMEM((LANES, trunc), BF16),
             pltpu.VMEM((lat_all, LANES), F32),
@@ -359,24 +391,23 @@
             pltpu.VMEM(by_z, BF16),
             pltpu.VMEM(by_d, BF16),
             pltpu.VMEM(by_d, BF16),
-            pltpu.VMEM(by_d, BF16),
-            pltpu.VMEM(by_d, BF16),
-            pltpu.VMEM(by_z, BF16),
-            pltpu.VMEM(by_z, BF16),
+            pltpu.VMEM((waves, 2, LANES), BF16),
+            pltpu.VMEM((waves, 2, LANES), BF16),
             pltpu.VMEM((2, 16, lat_all // 2), BF16),
             pltpu.VMEM((ys, 2, 16, lat_all // 2), BF16),
-            pltpu.VMEM((levels_all, 4 * levels_all), F32),
-            pltpu.VMEM((ys, levels_all, 4 * levels_all), F32),
+            pltpu.VMEM((LEVS, LANES), F32),
+            pltpu.VMEM((ys, LEVS, LANES), F32),
+            pltpu.SemaphoreType.DMA((8,)),
             pltpu.SemaphoreType.DMA((XS,)),
-            pltpu.SemaphoreType.DMA((6,)),
-            pltpu.SemaphoreType.DMA((6,)),
+            pltpu.SemaphoreType.DMA((5,)),
+            pltpu.SemaphoreType.DMA((5,)),
         ],
         compiler_params=pltpu.CompilerParams(
-            collective_id=0, has_side_effects=True, vmem_limit_bytes=48 * 1024 * 1024
+            collective_id=0, has_side_effects=True, vmem_limit_bytes=60 * 1024 * 1024
         ),
     )(
-        spec_in, legendre, wavenum.reshape(1, -1), wavenum, counts, quad_weights, mode_rates,
-        vert_in, vert_out,
+        spec_in, legendre, wavenum, wavenum.reshape(1, -1), counts, quad_weights, mode_rates,
+        vert_in.T, vert_out,
     )
 
 

time: 55.9 us -> 45.3 us (0.81)
  local copies, waits for them, and re-layouts: 6.93 us -> 1.56 us
  Pallas kernels: 48.7 us -> 43.5 us
    unnamed x16 -> x1, local copies, waits for them, and re-layouts: 6.93 us -> 1.56 us
    pallas_call x1, Pallas kernels: 48.7 us -> 43.5 us  [body(): pl.pallas_call(functools.partial(kernel, zs, ys), out_shape=jax.ShapeDtyp...]
where the time goes in v2:
time: 45.3 us; the launch traced here: 45.1 us
  Pallas kernels  43.5 us (96%)
  local copies, waits for them, and re-layouts  1.56 us (3%)
    pallas_call x1, Pallas kernels, body(): pl.pallas_call(functools.partial(kernel, zs, ys), out_shape=jax.ShapeDtyp...  43.5 us
    unnamed x1, local copies, waits for them, and re-layouts  1.56 us

profile of v2, /device:TPU:1, one launch (start us, length us, event | category | flops | bytes accessed | tf_op | source)
XLA Modules:
  0.0 45.1 jit_solution(3230040064308597066)
XLA Ops:
  0.0 43.5 %shard_map.82 = bf16[1,48,1280]{2,1,0:T(8,128)(2,1)} custom-call(bf16[1,48,1280]{2,1,0:T(8,128)(2,1)} %spec_hbm.1, bf16[1,512,1280]{2,1,0:T(8,128)(2,1)} %leg_hbm.1, s32[128]{0:T(128)} %wav_hbm.1, s32[1,128]{1,0:T(1,128)} %bitcast.3, s32[4]{0:T(128)} %counts_hbm.1, f32[4]{0:T(128)} %weights_hbm.1, f32[32]{0:T(128)} %rates_hbm.1, f32[8,32]{1,0:T(8,128)} %bitcast.2, ...), custom_call_target="tpu_custom_call" | custom-call | tf_op jit(solution)/shard_map/pallas_call | solution.py:367
  43.5 1.6 %copy.10 = bf16[1,48,1280]{2,1,0:T(8,128)(2,1)} copy(bf16[1,48,1280]{2,1,0:T(8,128)(2,1)} %shard_map.82) | data formatting | bytes 245760

commit v3 on v2

--- a/solution.py
+++ b/solution.py
@@ -62,9 +62,9 @@
     zs, ys, spec_hbm, leg_hbm, wav_hbm, wav_row_hbm, counts_hbm, weights_hbm, rates_hbm, vin_hbm, vout_hbm,
     out_ref,
     spec_ref, wav_row, vin_ref, vout_ref, wav_s, counts_s, weights_s, rates_s,
-    leg, spec2, fou, stage, wcol, table, lp, inv, out32,
-    s1_out, s1_in, s2_out, s2_in, b_out, b_in, y_out, y_in, v_out, v_in,
-    load_sem, leg_sem, send_sem, recv_sem,
+    leg, spec2, fou, stage, stage_back, wcol, table, table_back, lp, inv, out32,
+    a_out, a_in, b_out, b_in, y_out, y_in, v_out, v_in,
+    load_sem, leg_sem, send_sem, recv_sem, all_in,
 ):
     ds = XS * CORES
     waves = ds * zs
@@ -82,10 +82,13 @@
     def device(to_x, to_z, to_core):
         return (to_x * (zs * CORES) + to_z * CORES + to_core, y)
 
+    def ring_away(i):
+        odd = i % 2
+        return odd * (zs // 2 - (i + 1) // 2) + (1 - odd) * (zs // 2 + i // 2)
+
     z_peers = []
     for i in range(zs - 1):
-        away = zs // 2 - (i + 1) // 2 if i % 2 else zs // 2 + i // 2
-        to = (z + away) % zs
+        to = (z + ring_away(i)) % zs
         z_peers.append((to, device(x, to, core)))
     d_away = [(k, c) for k in sorted(range(XS), key=lambda k: -min(k, XS - k)) for c in range(CORES)]
     d_peers = []
@@ -94,7 +97,7 @@
         if (k, c) != (0, 0):
             d_peers.append((to_x * CORES + to_core, device(to_x, z, to_core)))
     y_peers = []
-    for k in range(1, ys):
+    for k in sorted(range(1, ys), key=lambda k: -min(k, ys - k)):
         to = (y + k) % ys
         y_peers.append((to, (me, to)))
 
@@ -148,17 +151,40 @@
         leg_loads[k].wait()
         rows = pl.ds(k * part_rows, part_rows)
         fou[rows] = dot_rows(leg[rows], spec2[...])
-
-    first_half = iota((LATS, LANES), 1) < HALF
-    for to in range(zs):
-        for k in range(XS):
-            low = fou[pl.ds(k * part_rows + 8 * to, 4, stride=2)]
-            high = fou[pl.ds(k * part_rows + 8 * to + 1, 4, stride=2)]
-            stage[pl.ds(to * 4 * XS + 4 * k, 4)] = jnp.where(first_half, low, high)
-    s1_out[...] = stage[...].astype(BF16).reshape(s1_out.shape)
+    first_half = iota((lat_all // 2, LANES), 1) < HALF
+    low = fou[pl.ds(0, lat_all // 2, stride=2)]
+    high = fou[pl.ds(1, lat_all // 2, stride=2)]
+    a_out[...] = jnp.where(first_half, low, high).astype(BF16).reshape(a_out.shape)
+
+    def push(number, leave, arrive, to_x, to_z, to_core):
+        to = device(to_x, to_z, to_core)
+        pltpu.make_async_remote_copy(
+            src_ref=leave.at[to[0]], dst_ref=arrive.at[me],
+            send_sem=send_sem.at[number], recv_sem=recv_sem.at[number],
+            device_id=to, device_id_type=MESH,
+        ).start()
+
+    def push_ring(number, leave, arrive, pairs, own):
+        def push_pairs(away, some):
+            for k, c in some:
+                push(number, leave, arrive, (x + k) % XS, (z + away) % zs, (core + c) % CORES)
+
+        def one(i, carry):
+            push_pairs(ring_away(i), pairs)
+            return carry
+
+        lax.fori_loop(0, zs - 1, one, 0)
+        push_pairs(0, own)
+
+    others_here = [pair for pair in d_away if pair != (0, 0)]
 
     pl.semaphore_wait(barrier, len(z_peers) + len(d_peers) + len(y_peers))
-    send(0, lambda slot: s1_out.at[slot], s1_in, z, z_peers)
+    for _, to in d_peers:
+        pl.semaphore_signal(all_in, inc=1, device_id=to, device_id_type=MESH)
+    push_ring(0, a_out, a_in, [(0, 0)], [])
+    pltpu.make_async_copy(a_out.at[me], a_in.at[me], recv_sem.at[0]).start()
+    pl.semaphore_wait(all_in, len(d_peers))
+    push_ring(0, a_out, a_in, others_here, others_here)
 
     for load in loads[2:]:
         load.wait()
@@ -169,18 +195,15 @@
 
     place = iota((waves, waves), 0)
     across = iota((waves, waves), 1)
-    natural = (place // (CORES * zs)) * (CORES * zs) + (place % zs) * CORES + (place // zs) % CORES
-    waves_f = wav_row[...].astype(F32)
-    column = jnp.sum(jnp.where(across == natural, waves_f, 0.0), axis=1, keepdims=True)
-    row = jnp.sum(jnp.where(across == place, column, 0.0), axis=0, keepdims=True)
+    row = wav_row[...].astype(F32)
     even = row - 2.0 * jnp.floor(row * 0.5) == 0.0
     parity = jnp.where(even, 1.0, -1.0)
+    column = jnp.sum(jnp.where(across == place, row, 0.0), axis=1, keepdims=True)
     wcol[...] = jnp.broadcast_to(column, wcol.shape)
-
-    chunk = waves // 4
 
     def table_part(step, carry):
         lat = step // 4
+        chunk = waves // 4
         begin = pl.multiple_of((step % 4) * chunk, chunk)
         count = jnp.full((chunk, LANES), counts_s[lat].astype(F32), F32)
         per_count = 1.0 / count
@@ -197,25 +220,36 @@
 
     lax.fori_loop(0, LATS * 4, table_part, 0)
 
-    arrived(0, s1_in)
-    stage[...] = s1_in[...].astype(F32).reshape(stage.shape)
-    slots = 4 * XS
-    first_half = iota((zs, LANES), 1) < HALF
-    for k in range(ds):
-        for t in range(2):
-            s2_out[k, t] = stage[pl.ds(2 * k + t, zs, stride=slots)].astype(BF16)
-    send(1, lambda slot: s2_out.at[slot], s2_in, d, d_peers)
+    def back_part(step, carry):
+        lat = step // 4
+        chunk = LANES // 4
+        begin = pl.multiple_of((step % 4) * chunk, chunk)
+        count = jnp.full((chunk, waves), counts_s[lat].astype(F32), F32)
+        per_count = 1.0 / count
+        quarter = counts_s[lat] // 4
+        offset = (iota((chunk, waves), 0) + begin).astype(F32)
+        c, s = turn(row * offset, count, per_count)
+        step_c, step_s = turn(jnp.broadcast_to(row * float(LANES), (chunk, waves)), count, per_count)
+        for a in range(points // LANES):
+            at = pl.ds(a * LANES + begin, chunk)
+            j = iota((chunk, waves), 0) + (a * LANES + begin)
+            share = jnp.where((j == 0) | (j == quarter), 0.5, jnp.where(j > quarter, 0.0, 1.0))
+            table_back[lat, at, 0:waves] = (c * share).astype(BF16)
+            table_back[lat, at, waves:] = (s * share).astype(BF16)
+            c, s = c * step_c - s * step_s, s * step_c + c * step_s
+        return carry
+
+    lax.fori_loop(0, LATS * 4, back_part, 0)
 
     r = iota((LANES, LANES), 0)
     field = (r // LEVS) % 4
     wanted = (r // HALF) * HALF + (r % LEVS) * 6 + 2 * field + (r // 32) % 2
     pick = jnp.where((iota((LANES, LANES), 1) == wanted) & (field < 3), 1.0, 0.0).astype(BF16)
 
-    arrived(1, s2_in)
 
     def grid_pair(t):
-        got = s2_in[:, t].reshape(waves, LANES)
-        coeffs = dot_rows(pick, got)
+        got = stage[pl.ds(t, waves, stride=2)].astype(BF16)
+        coeffs = dot_rows(pick, got) * (1.0 / math.sqrt(2 * waves))
         blocks = []
         for low in range(2):
             lat = 2 * t + low
@@ -232,19 +266,15 @@
                 ],
                 0,
             ).astype(BF16)
-            grid = dot(w, table[lat]) * (1.0 / math.sqrt(2 * waves))
+            grid = dot(w, table[lat])
             count = counts_s[lat]
-            quarter = count // 4
-            j = iota((1, points), 1)
-            share = jnp.where((j == 0) | (j == quarter), 0.5, 1.0)
-            share = jnp.where(j > quarter, 0.0, share)
             tend = []
             for q in range(4):
                 g = [grid[q * 24 + f * 8 : q * 24 + f * 8 + 8] for f in range(FIELDS)]
                 tend.append([g[0] - g[1] * g[2], g[1] + g[0] * g[2], g[2] - g[0] * g[1]])
             folded = [[], [], [], []]
             for f in range(FIELDS):
-                t0, t1, t2, t3 = (tend[q][f] * share for q in range(4))
+                t0, t1, t2, t3 = (tend[q][f] for q in range(4))
                 plus, minus = t0 + t1, t0 - t1
                 plus_far, minus_far = t2 + t3, t2 - t3
                 folded[0].append(plus + plus_far)
@@ -252,7 +282,7 @@
                 folded[2].append(minus + minus_far)
                 folded[3].append(minus - minus_far)
             u = jnp.concatenate(folded[0] + folded[1] + folded[2] + folded[3], 0).astype(BF16)
-            back = dot_rows(u, table[lat])
+            back = dot(u, table_back[lat])
             count_f = jnp.full((1, waves), count.astype(F32), F32)
             factor = jnp.full((1, waves), weights_s[lat], F32) / jnp.sqrt(count_f)
             cos_out = jnp.where(even, back[0:24, :waves], back[24:48, :waves]) * factor
@@ -262,29 +292,15 @@
                 blocks.append(sin_out[f * 8 : f * 8 + 8])
             blocks.append(jnp.zeros((16, waves), F32))
         returned = jnp.concatenate(blocks, 0).astype(BF16)
-        stage[pl.ds(t, waves, stride=2)] = dot_rows(unit(waves), returned)
-
+        stage_back[pl.ds(t, waves, stride=2)] = dot_rows(unit(waves), returned)
+
+    arrived(0, a_in)
+    stage[...] = a_in[...].astype(F32).reshape(stage.shape)
     for t in range(2):
         grid_pair(t)
-    b_out[...] = stage[...].astype(BF16).reshape(b_out.shape)
-    def send_back(away, pairs):
-        to_z = (z + away) % zs
-        for k, c in pairs:
-            to_x, to_core = (x + k) % XS, (core + c) % CORES
-            pltpu.make_async_remote_copy(
-                src_ref=b_out.at[(to_x * CORES + to_core) * zs + to_z], dst_ref=b_in.at[me],
-                send_sem=send_sem.at[2], recv_sem=recv_sem.at[2],
-                device_id=device(to_x, to_z, to_core), device_id_type=MESH,
-            ).start()
-
-    def send_ring(i, carry):
-        odd = i % 2
-        send_back(odd * (zs // 2 - (i + 1) // 2) + (1 - odd) * (zs // 2 + i // 2), d_away)
-        return carry
-
-    lax.fori_loop(0, zs - 1, send_ring, 0)
-    send_back(0, [pair for pair in d_away if pair != (0, 0)])
-    pltpu.make_async_copy(b_out.at[d * zs + z], b_in.at[me], recv_sem.at[2]).start()
+    b_out[...] = stage_back[...].astype(BF16).reshape(b_out.shape)
+    push_ring(3, b_out, b_in, d_away, others_here)
+    pltpu.make_async_copy(b_out.at[me], b_in.at[me], recv_sem.at[3]).start()
 
     target = iota((1, lat_all), 1)
     line = iota((lat_all // 2, lat_all), 0)
@@ -304,14 +320,13 @@
     whole = v_in[...].reshape(levels_all, LANES)
     whole_high = whole.astype(BF16).astype(F32)
     whole_low = whole - whole_high
-    into = jnp.concatenate([whole_high, whole_high, whole_low, whole_low], 0).astype(BF16)
-    into = dot_rows(unit(LANES), into)[0:levels_all].astype(BF16)
-    lane = iota((LEVS, 4 * levels_all), 1)
-    whole = jnp.zeros((LEVS, 4 * levels_all), F32)
-    for k in range(levels_all):
-        whole = jnp.where(lane % levels_all == k, vout_ref[:, k : k + 1], whole)
+    into = dot_rows(unit(LANES), jnp.concatenate([whole_high, whole_low], 0).astype(BF16))
+    into = jnp.concatenate([into[0:levels_all, 0:levels_all], into[0:levels_all, levels_all:]], 0)
+    into = jnp.concatenate([into, into], 1).astype(BF16)
+    whole = vout_ref[...]
     whole_high = whole.astype(BF16).astype(F32)
-    onto = jnp.where(lane < 2 * levels_all, whole_high, whole - whole_high).astype(BF16)
+    onto = jnp.concatenate([whole_high, whole - whole_high], 0)
+    onto = jnp.concatenate([onto, onto], 1).astype(BF16)
 
     def place_rows(begin, value):
         for a in range(trunc // LANES):
@@ -320,13 +335,17 @@
     def high_low(value):
         high = value.astype(BF16)
         low = (value - high.astype(F32)).astype(BF16)
-        return jnp.concatenate([high, low, high, low], 0)
-
-    arrived(2, b_in)
+        return jnp.concatenate([high, low], 0)
+
+    def times(twice, value):
+        both = dot(twice, high_low(value))
+        return both[: both.shape[0] // 2] + both[both.shape[0] // 2 :]
+
+    arrived(3, b_in)
     back = dot_rows(unit(LANES), b_in[...].reshape(lat_all // 2, LANES)).astype(BF16)
-    y_out[0] = back[0:16]
-    y_out[1] = back[HALF : HALF + 16]
-    send(3, lambda slot: y_out, y_in, y, y_peers)
+    for low in range(2):
+        y_out[low] = back[low * HALF : low * HALF + 16]
+        send(5 + low, lambda slot, low=low: y_out.at[low], y_in.at[low], y, y_peers)
     others = dot(back[16:48], lp[0]) + dot(back[HALF + 16 : HALF + 48], lp[1])
     others = jnp.where(kept, others, 0.0)
     for f in (1, 2):
@@ -334,24 +353,24 @@
             begin = (f - 1) * 16 + part * 8
             place_rows(2 * f + part, others[begin : begin + LEVS])
 
-    arrived(3, y_in)
-    first = y_in[:, 0].reshape(ys * 16, lat_all // 2)
-    second = y_in[:, 1].reshape(ys * 16, lat_all // 2)
-    diverg = dot(first, lp[0]) + dot(second, lp[1])
+    arrived(5, y_in.at[0])
+    diverg = dot(y_in[0].reshape(ys * 16, lat_all // 2), lp[0])
+    arrived(6, y_in.at[1])
+    diverg = diverg + dot(y_in[1].reshape(ys * 16, lat_all // 2), lp[1])
     diverg = jnp.where(kept, diverg, 0.0)
     for part in range(2):
         of_part = [diverg[k * 16 + part * 8 : k * 16 + part * 8 + 8] for k in range(ys)]
-        modes = dot(into, high_low(jnp.concatenate(of_part, 0)))
-        solved = dot(onto, high_low(modes * inv[...]))
+        modes = times(into, jnp.concatenate(of_part, 0))
+        solved = times(onto, modes * inv[...])
         place_rows(part, solved)
     for a in range(trunc // LANES):
         out_ref[0, :, a * LANES : (a + 1) * LANES] = out32[a].astype(BF16)
 
-    sent(0, s1_in, zs - 1)
-    sent(1, s2_in, ds - 1)
-    sent(2, b_in, waves - 1)
-    sent(3, y_in, ys - 1)
+    sent(0, a_in, waves - 1)
+    sent(3, b_in, waves - 1)
     sent(4, v_in, ys - 1)
+    sent(5, y_in.at[0], ys - 1)
+    sent(6, y_in.at[1], ys - 1)
 
 
 def body(spec_in, legendre, wavenum, counts, quad_weights, vert_in, vert_out, mode_rates, zs, ys):
@@ -362,11 +381,9 @@
     levels_all = ys * LEVS
     points = -(-(PTS // 4 + 1) // LANES) * LANES
     any_place = pl.BlockSpec(memory_space=pl.ANY)
-    by_z = (zs, 4 * XS, LANES)
-    by_d = (ds, 2, zs, LANES)
     return pl.pallas_call(
         functools.partial(kernel, zs, ys),
-        out_shape=jax.ShapeDtypeStruct((1, columns, trunc), BF16),
+        out_shape=pltpu.VMEM((1, columns, trunc), BF16),
         in_specs=[any_place] * 9,
         out_specs=pl.BlockSpec(memory_space=pltpu.VMEM),
         scratch_shapes=[
@@ -382,25 +399,26 @@
             pltpu.VMEM((LANES, trunc), BF16),
             pltpu.VMEM((lat_all, LANES), F32),
             pltpu.VMEM((lat_all // 2, LANES), F32),
+            pltpu.VMEM((lat_all // 2, LANES), F32),
             pltpu.VMEM((waves, LANES), F32),
             pltpu.VMEM((LATS, 2 * waves, points), BF16),
+            pltpu.VMEM((LATS, points, 2 * waves), BF16),
             pltpu.VMEM((2, lat_all // 2, trunc), BF16),
             pltpu.VMEM((levels_all, trunc), F32),
             pltpu.VMEM((trunc // LANES, columns, LANES), F32),
-            pltpu.VMEM(by_z, BF16),
-            pltpu.VMEM(by_z, BF16),
-            pltpu.VMEM(by_d, BF16),
-            pltpu.VMEM(by_d, BF16),
+            pltpu.VMEM((waves, 2, LANES), BF16),
+            pltpu.VMEM((waves, 2, LANES), BF16),
             pltpu.VMEM((waves, 2, LANES), BF16),
             pltpu.VMEM((waves, 2, LANES), BF16),
             pltpu.VMEM((2, 16, lat_all // 2), BF16),
-            pltpu.VMEM((ys, 2, 16, lat_all // 2), BF16),
+            pltpu.VMEM((2, ys, 16, lat_all // 2), BF16),
             pltpu.VMEM((LEVS, LANES), F32),
             pltpu.VMEM((ys, LEVS, LANES), F32),
             pltpu.SemaphoreType.DMA((8,)),
             pltpu.SemaphoreType.DMA((XS,)),
-            pltpu.SemaphoreType.DMA((5,)),
-            pltpu.SemaphoreType.DMA((5,)),
+            pltpu.SemaphoreType.DMA((7,)),
+            pltpu.SemaphoreType.DMA((7,)),
+            pltpu.SemaphoreType.REGULAR,
         ],
         compiler_params=pltpu.CompilerParams(
             collective_id=0, has_side_effects=True, vmem_limit_bytes=60 * 1024 * 1024

time: 45.3 us -> 43.1 us (0.951)
  Pallas kernels: 43.5 us -> 42.3 us
  local copies, waits for them, and re-layouts: 1.56 us -> 0.65 us
    pallas_call x1, Pallas kernels: 43.5 us -> 42.3 us  [body(): pl.pallas_call(functools.partial(kernel, zs, ys), out_shape=pltpu.VMEM((1...]
    unnamed x1, local copies, waits for them, and re-layouts: 1.56 us -> 0.65 us
where the time goes in v3:
time: 43.1 us; the launch traced here: 42.9 us
  Pallas kernels  42.3 us (98%)
  local copies, waits for them, and re-layouts  0.65 us (2%)
    pallas_call x1, Pallas kernels, body(): pl.pallas_call(functools.partial(kernel, zs, ys), out_shape=pltpu.VMEM((1...  42.3 us

profile of v3, /device:TPU:1, one launch (start us, length us, event | category | flops | bytes accessed | tf_op | source)
XLA Modules:
  0.0 42.9 jit_solution(1488570736666214903)
XLA Ops:
  0.0 42.3 %shard_map.82 = bf16[1,48,1280]{2,1,0:T(8,128)(2,1)S(1)} custom-call(bf16[1,48,1280]{2,1,0:T(8,128)(2,1)} %spec_hbm.1, bf16[1,512,1280]{2,1,0:T(8,128)(2,1)} %leg_hbm.1, s32[128]{0:T(128)} %wav_hbm.1, s32[1,128]{1,0:T(1,128)} %bitcast.3, s32[4]{0:T(128)} %counts_hbm.1, f32[4]{0:T(128)} %weights_hbm.1, f32[32]{0:T(128)} %rates_hbm.1, f32[8,32]{1,0:T(8,128)} %bitcast.2, ...), custom_call_target="tpu_custom_call" | custom-call | tf_op jit(solution)/shard_map/pallas_call | solution.py:384
  42.3 0.7 %copy.10 = bf16[1,48,1280]{2,1,0:T(8,128)(2,1)} copy(bf16[1,48,1280]{2,1,0:T(8,128)(2,1)S(1)} %shard_map.82) | data formatting | bytes 245760

commit v4 on v3

--- a/solution.py
+++ b/solution.py
@@ -247,57 +247,63 @@
     pick = jnp.where((iota((LANES, LANES), 1) == wanted) & (field < 3), 1.0, 0.0).astype(BF16)
 
 
-    def grid_pair(t):
-        got = stage[pl.ds(t, waves, stride=2)].astype(BF16)
-        coeffs = dot_rows(pick, got) * (1.0 / math.sqrt(2 * waves))
+    def synthesis(lat, coeffs):
+        begin = (lat % 2) * HALF
+        cosine = coeffs[begin : begin + 24]
+        sine = coeffs[begin + 32 : begin + 56]
+        turned = parity * cosine
+        turned_sine = parity * sine
+        w = jnp.concatenate(
+            [
+                jnp.concatenate([cosine, sine], 1),
+                jnp.concatenate([cosine, -sine], 1),
+                jnp.concatenate([turned, turned_sine], 1),
+                jnp.concatenate([turned, -turned_sine], 1),
+            ],
+            0,
+        ).astype(BF16)
+        return dot(w, table[lat])
+
+    def products(grid):
+        tend = []
+        for q in range(4):
+            g = [grid[q * 24 + f * 8 : q * 24 + f * 8 + 8] for f in range(FIELDS)]
+            tend.append([g[0] - g[1] * g[2], g[1] + g[0] * g[2], g[2] - g[0] * g[1]])
+        folded = [[], [], [], []]
+        for f in range(FIELDS):
+            t0, t1, t2, t3 = (tend[q][f] for q in range(4))
+            plus, minus = t0 + t1, t0 - t1
+            plus_far, minus_far = t2 + t3, t2 - t3
+            folded[0].append(plus + plus_far)
+            folded[1].append(plus - plus_far)
+            folded[2].append(minus + minus_far)
+            folded[3].append(minus - minus_far)
+        return jnp.concatenate(folded[0] + folded[1] + folded[2] + folded[3], 0).astype(BF16)
+
+    def analysis(lat, u):
+        back = dot(u, table_back[lat])
+        count_f = jnp.full((1, waves), counts_s[lat].astype(F32), F32)
+        factor = jnp.full((1, waves), weights_s[lat], F32) / jnp.sqrt(count_f)
+        cos_out = jnp.where(even, back[0:24, :waves], back[24:48, :waves]) * factor
+        sin_out = jnp.where(even, back[48:72, waves:], back[72:96, waves:]) * -factor
         blocks = []
-        for low in range(2):
-            lat = 2 * t + low
-            cosine = coeffs[low * HALF : low * HALF + 24]
-            sine = coeffs[low * HALF + 32 : low * HALF + 56]
-            turned = parity * cosine
-            turned_sine = parity * sine
-            w = jnp.concatenate(
-                [
-                    jnp.concatenate([cosine, sine], 1),
-                    jnp.concatenate([cosine, -sine], 1),
-                    jnp.concatenate([turned, turned_sine], 1),
-                    jnp.concatenate([turned, -turned_sine], 1),
-                ],
-                0,
-            ).astype(BF16)
-            grid = dot(w, table[lat])
-            count = counts_s[lat]
-            tend = []
-            for q in range(4):
-                g = [grid[q * 24 + f * 8 : q * 24 + f * 8 + 8] for f in range(FIELDS)]
-                tend.append([g[0] - g[1] * g[2], g[1] + g[0] * g[2], g[2] - g[0] * g[1]])
-            folded = [[], [], [], []]
-            for f in range(FIELDS):
-                t0, t1, t2, t3 = (tend[q][f] for q in range(4))
-                plus, minus = t0 + t1, t0 - t1
-                plus_far, minus_far = t2 + t3, t2 - t3
-                folded[0].append(plus + plus_far)
-                folded[1].append(plus - plus_far)
-                folded[2].append(minus + minus_far)
-                folded[3].append(minus - minus_far)
-            u = jnp.concatenate(folded[0] + folded[1] + folded[2] + folded[3], 0).astype(BF16)
-            back = dot(u, table_back[lat])
-            count_f = jnp.full((1, waves), count.astype(F32), F32)
-            factor = jnp.full((1, waves), weights_s[lat], F32) / jnp.sqrt(count_f)
-            cos_out = jnp.where(even, back[0:24, :waves], back[24:48, :waves]) * factor
-            sin_out = jnp.where(even, back[48:72, waves:], back[72:96, waves:]) * -factor
-            for f in range(FIELDS):
-                blocks.append(cos_out[f * 8 : f * 8 + 8])
-                blocks.append(sin_out[f * 8 : f * 8 + 8])
-            blocks.append(jnp.zeros((16, waves), F32))
-        returned = jnp.concatenate(blocks, 0).astype(BF16)
-        stage_back[pl.ds(t, waves, stride=2)] = dot_rows(unit(waves), returned)
+        for f in range(FIELDS):
+            blocks.append(cos_out[f * 8 : f * 8 + 8])
+            blocks.append(sin_out[f * 8 : f * 8 + 8])
+        return blocks + [jnp.zeros((16, waves), F32)]
 
     arrived(0, a_in)
     stage[...] = a_in[...].astype(F32).reshape(stage.shape)
+    coeffs = []
     for t in range(2):
-        grid_pair(t)
+        got = stage[pl.ds(t, waves, stride=2)].astype(BF16)
+        coeffs.append(dot_rows(pick, got) * (1.0 / math.sqrt(2 * waves)))
+    grids = [synthesis(lat, coeffs[lat // 2]) for lat in range(LATS)]
+    folds = [products(grid) for grid in grids]
+    blocks = [analysis(lat, folds[lat]) for lat in range(LATS)]
+    for t in range(2):
+        returned = jnp.concatenate(blocks[2 * t] + blocks[2 * t + 1], 0).astype(BF16)
+        stage_back[pl.ds(t, waves, stride=2)] = dot_rows(unit(waves), returned)
     b_out[...] = stage_back[...].astype(BF16).reshape(b_out.shape)
     push_ring(3, b_out, b_in, d_away, others_here)
     pltpu.make_async_copy(b_out.at[me], b_in.at[me], recv_sem.at[3]).start()
@@ -306,7 +312,7 @@
     line = iota((lat_all // 2, lat_all), 0)
     for low in range(2):
         pick_rows = jnp.where(target == 2 * line + low, 1.0, 0.0).astype(BF16)
-        lp[low] = dot(pick_rows, leg[...]).astype(BF16)
+        lp[low * (lat_all // 2) : (low + 1) * (lat_all // 2)] = dot(pick_rows, leg[...]).astype(BF16)
 
     degree = iota((1, trunc), 1).astype(F32)
     growth = degree * (degree + 1.0) / float(trunc * trunc)
@@ -343,34 +349,34 @@
 
     arrived(3, b_in)
     back = dot_rows(unit(LANES), b_in[...].reshape(lat_all // 2, LANES)).astype(BF16)
-    for low in range(2):
-        y_out[low] = back[low * HALF : low * HALF + 16]
-        send(5 + low, lambda slot, low=low: y_out.at[low], y_in.at[low], y, y_peers)
-    others = dot(back[16:48], lp[0]) + dot(back[HALF + 16 : HALF + 48], lp[1])
+    y_out[:, 0 : lat_all // 2] = back[0:16]
+    y_out[:, lat_all // 2 :] = back[HALF : HALF + 16]
+    send(5, lambda slot: y_out, y_in, y, y_peers)
+    others = dot(jnp.concatenate([back[16:48], back[HALF + 16 : HALF + 48]], 1), lp[...])
     others = jnp.where(kept, others, 0.0)
     for f in (1, 2):
         for part in range(2):
             begin = (f - 1) * 16 + part * 8
             place_rows(2 * f + part, others[begin : begin + LEVS])
 
-    arrived(5, y_in.at[0])
-    diverg = dot(y_in[0].reshape(ys * 16, lat_all // 2), lp[0])
-    arrived(6, y_in.at[1])
-    diverg = diverg + dot(y_in[1].reshape(ys * 16, lat_all // 2), lp[1])
+    arrived(5, y_in)
+    diverg = dot(y_in[...].reshape(ys * 16, lat_all), lp[...])
     diverg = jnp.where(kept, diverg, 0.0)
+    levels = [
+        jnp.concatenate([diverg[k * 16 + part * 8 : k * 16 + part * 8 + 8] for k in range(ys)], 0)
+        for part in range(2)
+    ]
+    modes = [times(into, value) for value in levels]
+    solved = [times(onto, value * inv[...]) for value in modes]
     for part in range(2):
-        of_part = [diverg[k * 16 + part * 8 : k * 16 + part * 8 + 8] for k in range(ys)]
-        modes = times(into, jnp.concatenate(of_part, 0))
-        solved = times(onto, modes * inv[...])
-        place_rows(part, solved)
+        place_rows(part, solved[part])
     for a in range(trunc // LANES):
         out_ref[0, :, a * LANES : (a + 1) * LANES] = out32[a].astype(BF16)
 
     sent(0, a_in, waves - 1)
     sent(3, b_in, waves - 1)
     sent(4, v_in, ys - 1)
-    sent(5, y_in.at[0], ys - 1)
-    sent(6, y_in.at[1], ys - 1)
+    sent(5, y_in, ys - 1)
 
 
 def body(spec_in, legendre, wavenum, counts, quad_weights, vert_in, vert_out, mode_rates, zs, ys):
@@ -403,15 +409,15 @@
             pltpu.VMEM((waves, LANES), F32),
             pltpu.VMEM((LATS, 2 * waves, points), BF16),
             pltpu.VMEM((LATS, points, 2 * waves), BF16),
-            pltpu.VMEM((2, lat_all // 2, trunc), BF16),
+            pltpu.VMEM((lat_all, trunc), BF16),
             pltpu.VMEM((levels_all, trunc), F32),
             pltpu.VMEM((trunc // LANES, columns, LANES), F32),
             pltpu.VMEM((waves, 2, LANES), BF16),
             pltpu.VMEM((waves, 2, LANES), BF16),
             pltpu.VMEM((waves, 2, LANES), BF16),
             pltpu.VMEM((waves, 2, LANES), BF16),
-            pltpu.VMEM((2, 16, lat_all // 2), BF16),
-            pltpu.VMEM((2, ys, 16, lat_all // 2), BF16),
+            pltpu.VMEM((16, lat_all), BF16),
+            pltpu.VMEM((ys, 16, lat_all), BF16),
             pltpu.VMEM((LEVS, LANES), F32),
             pltpu.VMEM((ys, LEVS, LANES), F32),
             pltpu.SemaphoreType.DMA((8,)),

time: 43.1 us -> 42.4 us (0.984)
  Pallas kernels: 42.3 us -> 41.7 us
    pallas_call x1, Pallas kernels: 42.3 us -> 41.7 us  [body(): pl.pallas_call(functools.partial(kernel, zs, ys), out_shape=pltpu.VMEM((1...]
where the time goes in v4:
time: 42.4 us; the launch traced here: 42.3 us
  Pallas kernels  41.7 us (98%)
  local copies, waits for them, and re-layouts  0.65 us (2%)
    pallas_call x1, Pallas kernels, body(): pl.pallas_call(functools.partial(kernel, zs, ys), out_shape=pltpu.VMEM((1...  41.7 us

profile of v4, /device:TPU:1, one launch (start us, length us, event | category | flops | bytes accessed | tf_op | source)
XLA Modules:
  0.0 42.3 jit_solution(6144153899753057871)
XLA Ops:
  0.0 41.7 %shard_map.82 = bf16[1,48,1280]{2,1,0:T(8,128)(2,1)S(1)} custom-call(bf16[1,48,1280]{2,1,0:T(8,128)(2,1)} %spec_hbm.1, bf16[1,512,1280]{2,1,0:T(8,128)(2,1)} %leg_hbm.1, s32[128]{0:T(128)} %wav_hbm.1, s32[1,128]{1,0:T(1,128)} %bitcast.3, s32[4]{0:T(128)} %counts_hbm.1, f32[4]{0:T(128)} %weights_hbm.1, f32[32]{0:T(128)} %rates_hbm.1, f32[8,32]{1,0:T(8,128)} %bitcast.2, ...), custom_call_target="tpu_custom_call" | custom-call | tf_op jit(solution)/shard_map/pallas_call | solution.py:390
  41.7 0.7 %copy.10 = bf16[1,48,1280]{2,1,0:T(8,128)(2,1)} copy(bf16[1,48,1280]{2,1,0:T(8,128)(2,1)S(1)} %shard_map.82) | data formatting | bytes 245760

commit v5 on v4

--- a/solution.py
+++ b/solution.py
@@ -294,16 +294,16 @@
 
     arrived(0, a_in)
     stage[...] = a_in[...].astype(F32).reshape(stage.shape)
-    coeffs = []
-    for t in range(2):
-        got = stage[pl.ds(t, waves, stride=2)].astype(BF16)
-        coeffs.append(dot_rows(pick, got) * (1.0 / math.sqrt(2 * waves)))
+    got = [stage[pl.ds(t, waves, stride=2)] for t in range(2)]
+    both = dot_rows(pick, jnp.concatenate(got, 0).astype(BF16)) * (1.0 / math.sqrt(2 * waves))
+    coeffs = [both[:, :waves], both[:, waves:]]
     grids = [synthesis(lat, coeffs[lat // 2]) for lat in range(LATS)]
     folds = [products(grid) for grid in grids]
     blocks = [analysis(lat, folds[lat]) for lat in range(LATS)]
+    returned = jnp.concatenate(blocks[0] + blocks[1] + blocks[2] + blocks[3], 0).astype(BF16)
+    turned_back = dot_rows(unit(waves), returned)
     for t in range(2):
-        returned = jnp.concatenate(blocks[2 * t] + blocks[2 * t + 1], 0).astype(BF16)
-        stage_back[pl.ds(t, waves, stride=2)] = dot_rows(unit(waves), returned)
+        stage_back[pl.ds(t, waves, stride=2)] = turned_back[:, t * LANES : (t + 1) * LANES]
     b_out[...] = stage_back[...].astype(BF16).reshape(b_out.shape)
     push_ring(3, b_out, b_in, d_away, others_here)
     pltpu.make_async_copy(b_out.at[me], b_in.at[me], recv_sem.at[3]).start()

time: 42.4 us -> 42.5 us (level)
  no operation moved by 1% of the time
where the time goes in v5:
time: 42.5 us; the launch traced here: 42.3 us
  Pallas kernels  41.7 us (98%)
  local copies, waits for them, and re-layouts  0.65 us (2%)
    pallas_call x1, Pallas kernels, body(): pl.pallas_call(functools.partial(kernel, zs, ys), out_shape=pltpu.VMEM((1...  41.7 us

profile of v5, /device:TPU:1, one launch (start us, length us, event | category | flops | bytes accessed | tf_op | source)
XLA Modules:
  0.0 42.3 jit_solution(5416725048008689044)
XLA Ops:
  0.0 41.7 %shard_map.82 = bf16[1,48,1280]{2,1,0:T(8,128)(2,1)S(1)} custom-call(bf16[1,48,1280]{2,1,0:T(8,128)(2,1)} %spec_hbm.1, bf16[1,512,1280]{2,1,0:T(8,128)(2,1)} %leg_hbm.1, s32[128]{0:T(128)} %wav_hbm.1, s32[1,128]{1,0:T(1,128)} %bitcast.3, s32[4]{0:T(128)} %counts_hbm.1, f32[4]{0:T(128)} %weights_hbm.1, f32[32]{0:T(128)} %rates_hbm.1, f32[8,32]{1,0:T(8,128)} %bitcast.2, ...), custom_call_target="tpu_custom_call" | custom-call | tf_op jit(solution)/shard_map/pallas_call | solution.py:390
  41.7 0.7 %copy.10 = bf16[1,48,1280]{2,1,0:T(8,128)(2,1)} copy(bf16[1,48,1280]{2,1,0:T(8,128)(2,1)S(1)} %shard_map.82) | data formatting | bytes 245760
